TPU v7x, 128 devices: a whole 4x4x4 slice. The times are simulated.
128 devices in a mesh: blk: 16 (over x, z_hi, core), act: 8 (over z_lo, y).
Axes of the slice: x: 4, y: 4, z: 4 (z_hi: 2, z_lo: 2; z = z_hi * 2 + z_lo), core: 2. Of those that a mesh axis runs over, the one named last changes fastest.
Arguments:
- field_pos: float32 [3, 98304], P(None, 'blk'), may hold values from -6 to 6
- field_vel: float32 [3, 98304], P(None, 'blk'), may hold values from -3 to 3
- field_acc: float32 [3, 98304], P(None, 'blk'), may hold values from -6 to 6
- field_jerk: float32 [3, 98304], P(None, 'blk'), may hold values from -6 to 6
- field_mass: float32 [98304], P('blk')
- levels: int32 [98304], P('blk'), may hold values from 0 to 3
- active_index: int32 [16, 8, 64], P('blk', 'act'), may hold values from 0 to 6143, as said below
- active_count: int32 [16, 8], P('blk', 'act'), may hold values from 1 to 64, 256 in all within a row
Outputs:
- updated: float32 [12, 16, 8, 64], P(None, 'blk', 'act')
Inputs may be any that keep to these rules, and one draw needn't show every extreme that they name: `active_index`: within one block b the 8 lists hold distinct stars, live slots and dead ones alike. `active_count`: in every block b the counts sum to exactly 256, and one device of each block has all 64 slots live.
All inputs are finite; a program needn't handle non-finite values.
Results may differ from a plain program's by a relative error of at most 0.0003.
Values sent between devices are 32-bit elements; how exact they have to be, the bound alone decides.
No kernel may reach another device: no remote copies, remote signals or barrier semaphores. Data moves between devices by JAX's collectives and lax.ppermute only.
A program may use at most 64 MiB of HBM per device.

v0:
```python
import jax
import jax.numpy as jnp
from jax import lax
from jax.sharding import PartitionSpec as P

soften_sq = 0.01
now_ticks = 11
tick_length = 0.0625


def predict(pos, vel, acc, jerk, levels):
    period = jnp.left_shift(jnp.ones_like(levels), 4 - levels)
    elapse = (
        jnp.remainder(jnp.full_like(levels, now_ticks), period).astype(jnp.float32) * tick_length
    )
    pred_pos = pos + elapse * (vel + elapse * (acc / 2.0 + elapse * jerk / 6.0))
    pred_vel = vel + elapse * (acc + elapse * jerk / 2.0)
    return (pred_pos, pred_vel, elapse)


def pair_terms(act_pos, act_vel, src_pos, src_vel, src_mass):
    offset = src_pos[:, None, :] - act_pos[:, :, None]
    relvel = src_vel[:, None, :] - act_vel[:, :, None]
    dist_sq = jnp.sum(offset * offset, axis=0) + soften_sq
    inverse = lax.rsqrt(dist_sq)
    inv_sq = inverse * inverse
    strength = src_mass[None, :] * inverse * inv_sq
    radial = 3.0 * jnp.sum(offset * relvel, axis=0) * inv_sq
    new_acc = jnp.sum(strength * offset, axis=-1)
    new_jerk = jnp.sum(strength * (relvel - radial * offset), axis=-1)
    return (new_acc, new_jerk)


def field_sweep(act_pos, act_vel, src_pos, src_vel, src_mass):
    total = src_pos.shape[1]
    width = min(512, total)

    def sweep_step(block_id, sums):
        start = block_id * width
        part_acc, part_jerk = pair_terms(
            act_pos,
            act_vel,
            lax.dynamic_slice_in_dim(src_pos, start, width, 1),
            lax.dynamic_slice_in_dim(src_vel, start, width, 1),
            lax.dynamic_slice_in_dim(src_mass, start, width, 0),
        )
        return (sums[0] + part_acc, sums[1] + part_jerk)

    zeros = jnp.zeros_like(act_pos)
    return lax.fori_loop(0, total // width, sweep_step, (zeros, zeros))


def correct(pred_pos, pred_vel, old_acc, old_jerk, new_acc, new_jerk, elapse):
    span = elapse[None, :]
    change = old_acc - new_acc
    snap_term = (-6.0 * change - span * (4.0 * old_jerk + 2.0 * new_jerk)) / (span * span)
    crackle = (12.0 * change + 6.0 * span * (old_jerk + new_jerk)) / (span * span * span)
    span_four = span * span * span * span
    new_pos = pred_pos + span_four / 24.0 * snap_term + span_four * span / 120.0 * crackle
    new_vel = pred_vel + span * span * span / 6.0 * snap_term + span_four / 24.0 * crackle
    return jnp.concatenate([new_pos, new_vel, new_acc, new_jerk], axis=0)


def on_device(
    field_pos, field_vel, field_acc, field_jerk, field_mass, levels, active_index, active_count
):
    pred_pos, pred_vel, elapse = predict(field_pos, field_vel, field_acc, field_jerk, levels)
    slots = active_index.shape[2]
    chosen = active_index.reshape(-1)
    act_pos = pred_pos[:, chosen]
    act_vel = pred_vel[:, chosen]
    every_pos, every_vel = (
        lax.all_gather(act_pos, "blk", axis=1, tiled=True),
        lax.all_gather(act_vel, "blk", axis=1, tiled=True),
    )
    part_acc, part_jerk = field_sweep(every_pos, every_vel, pred_pos, pred_vel, field_mass)
    new_acc, new_jerk = (
        lax.psum_scatter(part_acc, "blk", scatter_dimension=1, tiled=True),
        lax.psum_scatter(part_jerk, "blk", scatter_dimension=1, tiled=True),
    )
    result = correct(
        act_pos,
        act_vel,
        field_acc[:, chosen],
        field_jerk[:, chosen],
        new_acc,
        new_jerk,
        elapse[chosen],
    )
    slot_ids = jnp.arange(slots, dtype=jnp.int32)
    live_slot = slot_ids < active_count.reshape(())
    final = jnp.where(live_slot[None, :], result, jnp.zeros_like(result))
    return final.reshape(12, 1, 1, slots)


def solution(mesh):
    return jax.shard_map(
        on_device,
        mesh=mesh,
        in_specs=(
            P(None, "blk"),
            P(None, "blk"),
            P(None, "blk"),
            P(None, "blk"),
            P("blk"),
            P("blk"),
            P("blk", "act", None),
            P("blk", "act"),
        ),
        out_specs=P(None, "blk", "act", None),
        check_vma=False,
    )
```

profile of v0, /device:TPU:1, one launch (start us, length us, event | category | flops | bytes accessed | tf_op | source)
XLA Modules:
  0.0 275.0 jit_solution(5983216744335780822)
XLA Ops:
  11.1 26.4 %all-gather.3 = f32[16,64,3]{1,2,0:T(4,128)S(1)} all-gather(f32[1,64,3]{1,2,0:T(4,128)S(1)} %copy.145), channel_id=3, replica_groups=mesh['blk'=16,'act'=8] {'blk'}, dimensions={0}, use_global_device_ids=true | all-gather | bytes 13056 | tf_op jit(solution)/shard_map/all_gather | solution.py:74
  39.3 19.3 %all-gather.2 = f32[16,64,3]{1,2,0:T(4,128)S(1)} all-gather(f32[1,64,3]{1,2,0:T(4,128)S(1)} %copy.142), channel_id=2, replica_groups=mesh['blk'=16,'act'=8] {'blk'}, dimensions={0}, use_global_device_ids=true | all-gather | bytes 13056 | tf_op jit(solution)/shard_map/all_gather | solution.py:73
  58.7 75.9 %while.16 = (s32[]{:T(128)}, f32[3,1024]{1,0:T(4,128)S(1)}, f32[3,1024]{1,0:T(4,128)S(1)}, f32[6144]{0:T(1024)}, f32[3,6144]{1,0:T(4,128)S(1)}, /*index=5*/f32[3...) while((s32[]{:T(128)}, f32[3,1024]{1,0:T(4,128)S(1)}, ...), condition=%wide.region_5.6_spmd.clone, body=%wide.region_0.5_spmd.clone.sunk | while | flops 24123396 | bytes 16980160 | solution.py:50
  59.5 1.8 fusion.25
  62.1 3.0 %fusion.26 = (f32[3,1024]{1,0:T(4,128)S(1)}, f32[3,1024]{1,0:T(4,128)S(1)}) fusion(f32[1024,512]{1,0:T(8,128)S(1)} %get-tuple-element.308, f32[3,1024]{1,0:T(4,128)S(1)} %get-tuple-element.345, f32[3,512]{1,0:T(4,128)S(1)} %constant_dynamic-slice_fusion.4, f32[1024,512]{1,0:T(8,128)S(1)} %get-tuple-element.309, f32[3,1024]{1,0:T(4,128)S(1)} %get-tuple-element.343, ...), kind=kLoop, calls=%fused_computation.11.clone.1 | loop fusion | flops 12576768 | bytes 4255744 | tf_op jit(solution)/shard_map/while/body/eval_jaxpr/reduce_sum | solution.py:30
  65.9 1.8 fusion.25
  68.4 3.0 %fusion.26 = (f32[3,1024]{1,0:T(4,128)S(1)}, f32[3,1024]{1,0:T(4,128)S(1)}) fusion(f32[1024,512]{1,0:T(8,128)S(1)} %get-tuple-element.308, f32[3,1024]{1,0:T(4,128)S(1)} %get-tuple-element.345, f32[3,512]{1,0:T(4,128)S(1)} %constant_dynamic-slice_fusion.4, f32[1024,512]{1,0:T(8,128)S(1)} %get-tuple-element.309, f32[3,1024]{1,0:T(4,128)S(1)} %get-tuple-element.343, ...), kind=kLoop, calls=%fused_computation.11.clone.1 | loop fusion | flops 12576768 | bytes 4255744 | tf_op jit(solution)/shard_map/while/body/eval_jaxpr/reduce_sum | solution.py:30
  72.2 1.8 fusion.25
  74.7 3.0 %fusion.26 = (f32[3,1024]{1,0:T(4,128)S(1)}, f32[3,1024]{1,0:T(4,128)S(1)}) fusion(f32[1024,512]{1,0:T(8,128)S(1)} %get-tuple-element.308, f32[3,1024]{1,0:T(4,128)S(1)} %get-tuple-element.345, f32[3,512]{1,0:T(4,128)S(1)} %constant_dynamic-slice_fusion.4, f32[1024,512]{1,0:T(8,128)S(1)} %get-tuple-element.309, f32[3,1024]{1,0:T(4,128)S(1)} %get-tuple-element.343, ...), kind=kLoop, calls=%fused_computation.11.clone.1 | loop fusion | flops 12576768 | bytes 4255744 | tf_op jit(solution)/shard_map/while/body/eval_jaxpr/reduce_sum | solution.py:30
  81.0 3.0 %fusion.26 = (f32[3,1024]{1,0:T(4,128)S(1)}, f32[3,1024]{1,0:T(4,128)S(1)}) fusion(f32[1024,512]{1,0:T(8,128)S(1)} %get-tuple-element.308, f32[3,1024]{1,0:T(4,128)S(1)} %get-tuple-element.345, f32[3,512]{1,0:T(4,128)S(1)} %constant_dynamic-slice_fusion.4, f32[1024,512]{1,0:T(8,128)S(1)} %get-tuple-element.309, f32[3,1024]{1,0:T(4,128)S(1)} %get-tuple-element.343, ...), kind=kLoop, calls=%fused_computation.11.clone.1 | loop fusion | flops 12576768 | bytes 4255744 | tf_op jit(solution)/shard_map/while/body/eval_jaxpr/reduce_sum | solution.py:30
  87.4 3.0 %fusion.26 = (f32[3,1024]{1,0:T(4,128)S(1)}, f32[3,1024]{1,0:T(4,128)S(1)}) fusion(f32[1024,512]{1,0:T(8,128)S(1)} %get-tuple-element.308, f32[3,1024]{1,0:T(4,128)S(1)} %get-tuple-element.345, f32[3,512]{1,0:T(4,128)S(1)} %constant_dynamic-slice_fusion.4, f32[1024,512]{1,0:T(8,128)S(1)} %get-tuple-element.309, f32[3,1024]{1,0:T(4,128)S(1)} %get-tuple-element.343, ...), kind=kLoop, calls=%fused_computation.11.clone.1 | loop fusion | flops 12576768 | bytes 4255744 | tf_op jit(solution)/shard_map/while/body/eval_jaxpr/reduce_sum | solution.py:30
  91.2 1.8 fusion.25
  93.7 3.0 %fusion.26 = (f32[3,1024]{1,0:T(4,128)S(1)}, f32[3,1024]{1,0:T(4,128)S(1)}) fusion(f32[1024,512]{1,0:T(8,128)S(1)} %get-tuple-element.308, f32[3,1024]{1,0:T(4,128)S(1)} %get-tuple-element.345, f32[3,512]{1,0:T(4,128)S(1)} %constant_dynamic-slice_fusion.4, f32[1024,512]{1,0:T(8,128)S(1)} %get-tuple-element.309, f32[3,1024]{1,0:T(4,128)S(1)} %get-tuple-element.343, ...), kind=kLoop, calls=%fused_computation.11.clone.1 | loop fusion | flops 12576768 | bytes 4255744 | tf_op jit(solution)/shard_map/while/body/eval_jaxpr/reduce_sum | solution.py:30
  100.0 3.0 %fusion.26 = (f32[3,1024]{1,0:T(4,128)S(1)}, f32[3,1024]{1,0:T(4,128)S(1)}) fusion(f32[1024,512]{1,0:T(8,128)S(1)} %get-tuple-element.308, f32[3,1024]{1,0:T(4,128)S(1)} %get-tuple-element.345, f32[3,512]{1,0:T(4,128)S(1)} %constant_dynamic-slice_fusion.4, f32[1024,512]{1,0:T(8,128)S(1)} %get-tuple-element.309, f32[3,1024]{1,0:T(4,128)S(1)} %get-tuple-element.343, ...), kind=kLoop, calls=%fused_computation.11.clone.1 | loop fusion | flops 12576768 | bytes 4255744 | tf_op jit(solution)/shard_map/while/body/eval_jaxpr/reduce_sum | solution.py:30
  106.3 3.0 %fusion.26 = (f32[3,1024]{1,0:T(4,128)S(1)}, f32[3,1024]{1,0:T(4,128)S(1)}) fusion(f32[1024,512]{1,0:T(8,128)S(1)} %get-tuple-element.308, f32[3,1024]{1,0:T(4,128)S(1)} %get-tuple-element.345, f32[3,512]{1,0:T(4,128)S(1)} %constant_dynamic-slice_fusion.4, f32[1024,512]{1,0:T(8,128)S(1)} %get-tuple-element.309, f32[3,1024]{1,0:T(4,128)S(1)} %get-tuple-element.343, ...), kind=kLoop, calls=%fused_computation.11.clone.1 | loop fusion | flops 12576768 | bytes 4255744 | tf_op jit(solution)/shard_map/while/body/eval_jaxpr/reduce_sum | solution.py:30
  112.7 3.0 %fusion.26 = (f32[3,1024]{1,0:T(4,128)S(1)}, f32[3,1024]{1,0:T(4,128)S(1)}) fusion(f32[1024,512]{1,0:T(8,128)S(1)} %get-tuple-element.308, f32[3,1024]{1,0:T(4,128)S(1)} %get-tuple-element.345, f32[3,512]{1,0:T(4,128)S(1)} %constant_dynamic-slice_fusion.4, f32[1024,512]{1,0:T(8,128)S(1)} %get-tuple-element.309, f32[3,1024]{1,0:T(4,128)S(1)} %get-tuple-element.343, ...), kind=kLoop, calls=%fused_computation.11.clone.1 | loop fusion | flops 12576768 | bytes 4255744 | tf_op jit(solution)/shard_map/while/body/eval_jaxpr/reduce_sum | solution.py:30
  116.4 1.8 fusion.25
  119.0 3.0 %fusion.26 = (f32[3,1024]{1,0:T(4,128)S(1)}, f32[3,1024]{1,0:T(4,128)S(1)}) fusion(f32[1024,512]{1,0:T(8,128)S(1)} %get-tuple-element.308, f32[3,1024]{1,0:T(4,128)S(1)} %get-tuple-element.345, f32[3,512]{1,0:T(4,128)S(1)} %constant_dynamic-slice_fusion.4, f32[1024,512]{1,0:T(8,128)S(1)} %get-tuple-element.309, f32[3,1024]{1,0:T(4,128)S(1)} %get-tuple-element.343, ...), kind=kLoop, calls=%fused_computation.11.clone.1 | loop fusion | flops 12576768 | bytes 4255744 | tf_op jit(solution)/shard_map/while/body/eval_jaxpr/reduce_sum | solution.py:30
  125.3 3.0 %fusion.26 = (f32[3,1024]{1,0:T(4,128)S(1)}, f32[3,1024]{1,0:T(4,128)S(1)}) fusion(f32[1024,512]{1,0:T(8,128)S(1)} %get-tuple-element.308, f32[3,1024]{1,0:T(4,128)S(1)} %get-tuple-element.345, f32[3,512]{1,0:T(4,128)S(1)} %constant_dynamic-slice_fusion.4, f32[1024,512]{1,0:T(8,128)S(1)} %get-tuple-element.309, f32[3,1024]{1,0:T(4,128)S(1)} %get-tuple-element.343, ...), kind=kLoop, calls=%fused_computation.11.clone.1 | loop fusion | flops 12576768 | bytes 4255744 | tf_op jit(solution)/shard_map/while/body/eval_jaxpr/reduce_sum | solution.py:30
  131.6 3.0 %fusion.26 = (f32[3,1024]{1,0:T(4,128)S(1)}, f32[3,1024]{1,0:T(4,128)S(1)}) fusion(f32[1024,512]{1,0:T(8,128)S(1)} %get-tuple-element.308, f32[3,1024]{1,0:T(4,128)S(1)} %get-tuple-element.345, f32[3,512]{1,0:T(4,128)S(1)} %constant_dynamic-slice_fusion.4, f32[1024,512]{1,0:T(8,128)S(1)} %get-tuple-element.309, f32[3,1024]{1,0:T(4,128)S(1)} %get-tuple-element.343, ...), kind=kLoop, calls=%fused_computation.11.clone.1 | loop fusion | flops 12576768 | bytes 4255744 | tf_op jit(solution)/shard_map/while/body/eval_jaxpr/reduce_sum | solution.py:30
  138.4 2.2 copy.140
  141.7 2.5 gather_fusion.2
  144.9 53.1 %reduce-scatter.9.cloned.1.call-done = f32[64,3]{1,0:T(8,128)} async-done(((f32[1024,3]{1,0:T(8,128)}), f32[64,3]{1,0:T(8,128)}) %reduce-scatter.9.cloned.1.call-update) | async-done | bytes 784
  198.9 67.8 %reduce-scatter.7.cloned.1.call-done = f32[64,3]{1,0:T(8,128)} async-done(((f32[1024,3]{1,0:T(8,128)}), f32[64,3]{1,0:T(8,128)}) %reduce-scatter.7.cloned.1.call-update) | async-done | bytes 784
  (111 shorter events, 44.5 us)
Async XLA Ops:
  6.5 191.5 %reduce-scatter.9.cloned.1.call-start = ((), (), s32[]{:S(2)}) async-start(), calls=%async_computation.3 | async-start | bytes 557056
  58.7 79.7 %copy-start = (f32[3,6144]{1,0:T(4,128)S(1)}, f32[3,6144]{1,0:T(4,128)}, u32[]{:S(2)}) copy-start(f32[3,6144]{1,0:T(4,128)} %param.12) | copy-start | bytes 221188
  134.6 6.0 %copy-start.1 = (f32[3,6144]{1,0:T(4,128)S(1)}, f32[3,6144]{1,0:T(4,128)}, u32[]{:S(2)}) copy-start(f32[3,6144]{1,0:T(4,128)} %param.13) | copy-start | bytes 221188
  135.7 130.9 %reduce-scatter.7.cloned.1.call-start = ((), (), s32[]{:S(2)}) async-start(), calls=%async_computation.2 | async-start | bytes 557056
Sparse Core Ops, SparseCore 0:
  135.8 62.1 reduce-scatter.8
  202.3 64.3 reduce-scatter.6
where the time goes:
time: 277 us; the launch traced here: 275 us
  waiting for transfers between devices  121 us (44%)
  other arithmetic  69.5 us (25%)
  blocking collectives  45.7 us (16%)
  local copies, waits for them, and re-layouts  24.1 us (9%)
  between operations  14.2 us (5%)
    unnamed x4, waiting for transfers between devices  121 us
    reduce_sum x12, other arithmetic, pair_terms(): new_jerk = jnp.sum(strength * (relvel - radial * offset), axis=-1)  35.6 us
    all_gather x1, blocking collectives, on_device(): lax.all_gather(act_vel, 'blk', axis=1, tiled=True)  26.4 us
    reduce_sum x12, other arithmetic, pair_terms(): radial = 3.0 * jnp.sum(offset * relvel, axis=0) * inv_sq  21.3 us
    all_gather x1, blocking collectives, on_device(): lax.all_gather(act_pos, 'blk', axis=1, tiled=True)  19.3 us
    dynamic_slice x12, local copies, waits for them, and re-layouts, sweep_step(): lax.dynamic_slice_in_dim(src_mass, start, width, 0)  9.2 us
    mul x12, other arithmetic, pair_terms(): strength = src_mass[None, :] * inverse * inv_sq  8.87 us
    unnamed x14, local copies, waits for them, and re-layouts  7.3 us
  transfers between devices with their start and end apart: 2, of which 2 were waited for; matrix products, arithmetic and copies ran while one was open for 3% of the time, Pallas kernels for 0%

commit v1 on v0

v1 whole, which is shorter than its diff:
```python
import functools

import jax
import jax.numpy as jnp
from jax import lax
from jax.experimental import pallas as pl
from jax.experimental.pallas import tpu as pltpu
from jax.sharding import PartitionSpec as P

F32 = jnp.float32
BF16 = jnp.bfloat16
SOFTEN = 0.01
NOW = 11
TICK = 0.0625
GRID = 16.0
LANES = 128
CAP = 64
STEP = 2048
VMEM = 44 << 20


def round_bf16(x):
    return x.astype(BF16).astype(F32)


def split2(x):
    a = round_bf16(x)
    return a, round_bf16(x - a)


def split3(x):
    a = round_bf16(x)
    b = round_bf16(x - a)
    return a, b, x - a - b


def coarse(x):
    c = round_bf16(jnp.round(x * GRID) * (1.0 / GRID))
    return c, x - c


def rows_sum(x):
    return jnp.sum(x, axis=0, keepdims=True)


def basis(p, v):
    c, d = coarse(p)
    e, f = coarse(v)
    parts = (c, *split2(d)), (e, *split2(f))
    norms = (
        rows_sum(c * c),
        rows_sum(2.0 * c * d + d * d),
        rows_sum(c * e),
        rows_sum(c * f + d * e + d * f),
    )
    return parts, norms


def select_kernel(
    idx_hbm, cnt_hbm, pos_hbm, vel_hbm, acc_hbm, jerk_hbm, mass_hbm, lev_hbm,
    send_ref, own_ref, pv_ref, idx, cnt, pos, vel, acc, jerk, mass, lev, table, sem,
):
    pairs = (
        (lev_hbm, lev), (pos_hbm, pos), (vel_hbm, vel), (acc_hbm, acc), (jerk_hbm, jerk), (mass_hbm, mass),
        (idx_hbm, idx), (cnt_hbm, cnt),
    )
    copies = [pltpu.make_async_copy(a, b, sem.at[k]) for k, (a, b) in enumerate(pairs)]
    for copy in copies:
        copy.start()
    for copy in copies:
        copy.wait()
    level = lev[...]
    period = jnp.left_shift(jnp.ones_like(level), 4 - level)
    e = lax.rem(jnp.full_like(level, NOW), period).astype(F32) * TICK
    x, u, a, j = pos[...], vel[...], acc[...], jerk[...]
    p = x + e * (u + e * (a * 0.5 + e * j / 6.0))
    v = u + e * (a + e * j * 0.5)
    pv_ref[0:3, :] = p
    pv_ref[3:6, :] = v
    pv_ref[6:7, :] = mass[...]
    table[0:3, :] = p
    table[3:6, :] = v
    table[6:9, :] = a
    table[9:12, :] = j
    table[12:13, :] = e
    lane = lax.broadcasted_iota(jnp.int32, (16, LANES), 1)
    got = jnp.zeros((16, LANES), F32)
    for s in range(CAP):
        i = idx[0, 0, s]
        block = table[:, pl.ds(pl.multiple_of((i >> 7) * LANES, LANES), LANES)]
        got = jnp.where(lane == s, pltpu.roll(block, (s - i) & (LANES - 1), 1), got)
    count = cnt[0, 0]
    own_ref[0:13, :] = got[0:13]
    own_ref[13:16, :] = jnp.full((3, LANES), count.astype(F32))
    row = lax.broadcasted_iota(jnp.int32, (8, LANES), 0)
    live = lax.broadcasted_iota(jnp.int32, (8, LANES), 1) < count
    out = jnp.where(row < 6, jnp.where(live, got[0:8], 0.0), jnp.where(row == 6, count.astype(F32), 0.0))
    for k in range(send_ref.shape[0]):
        send_ref[k] = out


def prepare_kernel(pv_ref, ys_ref, mt_ref, b_ref, m_ref):
    n = pv_ref.shape[1]
    p, v, m = pv_ref[0:3, :], pv_ref[3:6, :], pv_ref[6:7, :]
    (pp, vv), norms = basis(p, v)
    for k, x in enumerate((*pp, *vv)):
        b_ref[3 * k : 3 * k + 3, :] = x
    b_ref[18:20, :] = jnp.ones((2, n), F32)
    for k, x in enumerate(norms):
        for t, y in enumerate(split3(x)):
            b_ref[20 + 3 * k + t : 21 + 3 * k + t, :] = y
    m_ref[...] = jnp.zeros(m_ref.shape, F32)
    for k, x in enumerate((m * p, m * v)):
        for t, y in enumerate(split3(x)):
            m_ref[8 * t + 3 * k : 8 * t + 3 * k + 3, :] = y
    for t, y in enumerate(split3(m)):
        m_ref[8 * t + 6 : 8 * t + 7, :] = y
    mt_ref[...] = m_ref[...].astype(BF16)

    def body(i, _):
        o = pl.multiple_of(i * LANES, LANES)
        x = b_ref[:, pl.ds(o, LANES)].astype(BF16)
        ys_ref[pl.ds(o, LANES), :] = jnp.concatenate([x, x, x, x], axis=0).T
        return 0

    lax.fori_loop(0, n // LANES, body, 0, unroll=4)


def fill_weights(p, v, wq_ref, wr_ref):
    n = p.shape[1]
    (pp, vv), (cc, dn, ce, gn) = basis(p, v)
    wq_ref[...] = jnp.zeros(wq_ref.shape, F32)
    wr_ref[...] = jnp.zeros(wr_ref.shape, F32)
    cc, dn, ce, gn = split3(cc), split3(dn + SOFTEN), split3(ce), split3(gn)
    for w in range(3):
        o = 32 * w
        for k in range(3):
            wq_ref[o + 3 * k : o + 3 * k + 3, :] = -2.0 * pp[w]
            wr_ref[o + 3 * k : o + 3 * k + 3, :] = -vv[w]
            wr_ref[o + 9 + 3 * k : o + 12 + 3 * k, :] = -pp[w]
        wq_ref[o + 18 : o + 19, :] = cc[w]
        wq_ref[o + 19 : o + 20, :] = dn[w]
        wr_ref[o + 18 : o + 19, :] = ce[w]
        wr_ref[o + 19 : o + 20, :] = gn[w]
    wq_ref[20:26, :] = jnp.ones((6, n), F32)
    wr_ref[26:32, :] = jnp.ones((6, n), F32)


def sweep_kernel(recv_ref, ys_ref, mt_ref, out_ref, act_ref, res_ref, wq_ref, wr_ref, wqb_ref, wrb_ref):
    lists = recv_ref.shape[0]
    stars = ys_ref.shape[0]
    lane = lax.broadcasted_iota(jnp.int32, (8, LANES), 1)
    act_ref[...] = jnp.zeros(act_ref.shape, F32)
    offsets = []
    total = jnp.int32(0)
    for k in range(lists):
        x = recv_ref[k]
        offsets.append(total)
        shift = total & (LANES - 1)
        o = pl.multiple_of((total >> 7) * LANES, LANES)
        x = pltpu.roll(x, shift, 1)
        act_ref[:, pl.ds(o, LANES)] += jnp.where(lane >= shift, x, 0.0)
        act_ref[:, pl.ds(o + LANES, LANES)] += jnp.where(lane < shift, x, 0.0)
        total = total + jnp.max(recv_ref[k, 6:7, :].astype(jnp.int32))
    size = wq_ref.shape[1]
    fill_weights(act_ref[0:3, 0:size], act_ref[3:6, 0:size], wq_ref, wr_ref)
    wqb_ref[...] = wq_ref[...].astype(BF16)
    wrb_ref[...] = wr_ref[...].astype(BF16)

    def tile(a, width):
        cols = pl.ds(a, width)
        w = jnp.concatenate([wqb_ref[:, cols], wrb_ref[:, cols]], axis=1)

        def body(i, carry):
            high, low = carry
            o = pl.multiple_of(i * STEP, STEP)
            qr = jnp.dot(ys_ref[pl.ds(o, STEP), :], w, preferred_element_type=F32)
            q, rw = qr[:, :width], qr[:, width:]
            inv = lax.rsqrt(q)
            inv2 = inv * inv
            s = inv * inv2
            st = jnp.concatenate([s, s * inv2 * rw], axis=1)
            hi = st.astype(BF16)
            lo = (st - hi.astype(F32)).astype(BF16)
            high = high + jnp.dot(mt_ref[:, pl.ds(o, STEP)], hi, preferred_element_type=F32)
            low = low + jnp.dot(mt_ref[0:16, pl.ds(o, STEP)], lo, preferred_element_type=F32)
            return high, low

        zero = jnp.zeros((32, 2 * width), F32), jnp.zeros((16, 2 * width), F32)
        high, low = lax.fori_loop(0, stars // STEP, body, zero)
        x = (high[16:24] + low[8:16]) + (high[8:16] + low[0:8]) + high[0:8]
        s, t = x[:, :width], x[:, width:]
        p, v = act_ref[0:3, cols], act_ref[3:6, cols]
        res_ref[0:3, cols] = s[0:3] - p * s[6:7]
        res_ref[3:6, cols] = s[3:6] - v * s[6:7] - 3.0 * (t[0:3] - p * t[6:7])

    tiles = (total + (LANES - 1)) >> 7
    pairs = tiles >> 1

    def two(t, _):
        tile(pl.multiple_of(t * 2 * LANES, LANES), 2 * LANES)
        return 0

    def one(t, _):
        tile(pl.multiple_of(t * LANES, LANES), LANES)
        return 0

    lax.fori_loop(0, pairs, two, 0)
    lax.fori_loop(2 * pairs, tiles, one, 0)
    for k in range(lists):
        shift = offsets[k] & (LANES - 1)
        o = pl.multiple_of((offsets[k] >> 7) * LANES, LANES)
        back = (LANES - shift) & (LANES - 1)
        a = pltpu.roll(res_ref[:, pl.ds(o, LANES)], back, 1)
        b = pltpu.roll(res_ref[:, pl.ds(o + LANES, LANES)], back, 1)
        out_ref[k] = jnp.where(lane < LANES - shift, a, b)


def finish_kernel(recv_ref, own_ref, out_ref):
    x = recv_ref[0]
    for k in range(1, recv_ref.shape[0]):
        x = x + recv_ref[k]
    new_acc, new_jerk = x[0:3, :CAP], x[3:6, :CAP]
    own = own_ref[:, :CAP]
    p, v, acc, jerk, e = own[0:3], own[3:6], own[6:9], own[9:12], own[12:13]
    change = acc - new_acc
    e2 = e * e
    e3 = e2 * e
    e4 = e2 * e2
    snap = (-6.0 * change - e * (4.0 * jerk + 2.0 * new_jerk)) / e2
    crackle = (12.0 * change + 6.0 * e * (jerk + new_jerk)) / e3
    pos = p + e4 / 24.0 * snap + e4 * e / 120.0 * crackle
    vel = v + e3 / 6.0 * snap + e4 / 24.0 * crackle
    live = lax.broadcasted_iota(jnp.int32, (3, CAP), 1).astype(F32) < own[13:14]
    for k, y in enumerate((pos, vel, new_acc, new_jerk)):
        y = jnp.where(live, y, 0.0)
        for c in range(3):
            out_ref[3 * k + c, 0] = y[c : c + 1]


def spec(space):
    return pl.BlockSpec(memory_space=space)


def params(limit=VMEM):
    return pltpu.CompilerParams(vmem_limit_bytes=limit)


def on_device(groups, field_pos, field_vel, field_acc, field_jerk, field_mass, levels, active_index, active_count):
    n = field_pos.shape[1]
    lists = len(groups[0])
    vmem = spec(pltpu.VMEM)
    send, own, pv = pl.pallas_call(
        select_kernel,
        out_shape=(
            jax.ShapeDtypeStruct((lists, 8, LANES), F32),
            jax.ShapeDtypeStruct((16, LANES), F32),
            jax.ShapeDtypeStruct((8, n), F32),
        ),
        in_specs=[spec(pltpu.HBM)] * 8,
        scratch_shapes=[pltpu.SMEM((1, 1, CAP), jnp.int32), pltpu.SMEM((1, 1), jnp.int32)]
        + [pltpu.VMEM((3, n), F32)] * 4
        + [pltpu.VMEM((1, n), F32), pltpu.VMEM((1, n), jnp.int32), pltpu.VMEM((16, n), F32)]
        + [pltpu.SemaphoreType.DMA((8,))],
        compiler_params=params(60 << 20),
        cost_estimate=pl.CostEstimate(flops=1 << 20, bytes_accessed=1 << 20, transcendentals=0),
        name="select",
    )(
        active_index, active_count, field_pos, field_vel, field_acc, field_jerk,
        field_mass.reshape(1, n), levels.reshape(1, n),
    )
    axes = ("blk", "act")
    recv = lax.all_to_all(send, axes, 0, 0, axis_index_groups=groups, tiled=True)
    ys, mt = pl.pallas_call(
        prepare_kernel,
        out_shape=(jax.ShapeDtypeStruct((n, LANES), BF16), jax.ShapeDtypeStruct((32, n), BF16)),
        in_specs=[vmem],
        scratch_shapes=[pltpu.VMEM((32, n), F32)] * 2,
        compiler_params=params(),
        cost_estimate=pl.CostEstimate(flops=1 << 22, bytes_accessed=4 << 20, transcendentals=0),
        name="prepare",
    )(pv)
    size = lists * CAP
    part = pl.pallas_call(
        sweep_kernel,
        out_shape=jax.ShapeDtypeStruct((lists, 8, LANES), F32),
        in_specs=[vmem] * 3,
        scratch_shapes=[pltpu.VMEM((8, size + LANES), F32)] * 2
        + [pltpu.VMEM((LANES, size), F32)] * 2
        + [pltpu.VMEM((LANES, size), BF16)] * 2,
        compiler_params=params(),
        cost_estimate=pl.CostEstimate(flops=10 << 30, bytes_accessed=4 << 20, transcendentals=0),
        name="sweep",
    )(recv, ys, mt)
    back = lax.all_to_all(part, axes, 0, 0, axis_index_groups=groups, tiled=True)
    out = pl.pallas_call(
        finish_kernel,
        out_shape=jax.ShapeDtypeStruct((12, 1, 1, CAP), F32),
        in_specs=[vmem, vmem],
        compiler_params=params(),
        name="finish",
    )(back, own)
    return out


def list_groups():
    groups = []
    for y in range(4):
        for flip in range(2):
            group = []
            for b in range(16):
                z_hi = (b >> 1) & 1
                z_lo = z_hi ^ flip
                group.append(b * 8 + z_lo * 4 + y)
            groups.append(group)
    return groups


def solution(mesh):
    return jax.shard_map(
        functools.partial(on_device, list_groups()),
        mesh=mesh,
        in_specs=(
            P(None, "blk"),
            P(None, "blk"),
            P(None, "blk"),
            P(None, "blk"),
            P("blk"),
            P("blk"),
            P("blk", "act", None),
            P("blk", "act"),
        ),
        out_specs=P(None, "blk", "act", None),
        check_vma=False,
    )
```

time: 277 us -> 41.9 us (0.15)
  the two profiles are of different devices: /device:TPU:1 before, /device:TPU:17 now
where the time goes in v1:
time: 41.9 us; the launch traced here: 41.7 us
  Pallas kernels  17.8 us (42%)
  blocking collectives  9.96 us (24%)
  starting transfers between devices  8.47 us (20%)
  waiting for transfers between devices  3.86 us (9%)
  local copies, waits for them, and re-layouts  0.93 us (2%)
  between operations  0.68 us (2%)
    pallas_call x1, Pallas kernels, on_device(): pl.pallas_call(sweep_kernel, out_shape=jax.ShapeDtypeStruct((lists, 8, LA...  12.4 us
    all_to_all x1, blocking collectives, on_device(): lax.all_to_all(part, axes, 0, 0, axis_index_groups=groups, tiled=True)  9.96 us
    all_to_all x1, starting transfers between devices, on_device(): lax.all_to_all(send, axes, 0, 0, axis_index_groups=groups, tiled=True)  8.47 us
    all_to_all x1, waiting for transfers between devices, on_device(): lax.all_to_all(send, axes, 0, 0, axis_index_groups=groups, tiled=True)  3.86 us
    pallas_call x1, Pallas kernels, on_device(): pl.pallas_call(select_kernel, out_shape=(jax.ShapeDtypeStruct((lists, 8,...  2.48 us
    pallas_call x1, Pallas kernels, on_device(): pl.pallas_call(prepare_kernel, out_shape=(jax.ShapeDtypeStruct((n, LANES)...  2.28 us
    unnamed x4, local copies, waits for them, and re-layouts  0.93 us
  transfers between devices with their start and end apart: 1, of which 1 were waited for; matrix products, arithmetic and copies ran while one was open for 0% of the time, Pallas kernels for 5%

profile of v1, /device:TPU:17, one launch (start us, length us, event | category | flops | bytes accessed | tf_op | source)
XLA Modules:
  0.0 41.7 jit_solution(2101952042105840811)
XLA Ops:
  0.7 2.5 %select.1 = (f32[16,8,128]{2,1,0:T(8,128)}, f32[16,128]{1,0:T(8,128)}, f32[8,6144]{1,0:T(8,128)}) custom-call(s32[1,1,64]{2,1,0:T(1,128)} %idx_hbm.1, s32[1,1]{1,0:T(1,128)S(6)} %copy.9.cnt_hbm, f32[3,6144]{1,0:T(4,128)} %pos_hbm.1, f32[3,6144]{1,0:T(4,128)} %vel_hbm.1, f32[3,6144]{1,0:T(4,128)} %acc_hbm.1, f32[3,6144]{1,0:T(4,128)} %jerk_hbm.1, ...), custom_call_target="tpu_custom_call" | custom-call | flops 1048576 | bytes 1048576 | tf_op jit(solution)/shard_map/select/pallas_call | solution.py:253
  3.1 8.5 %all-to-all-start = ((f32[16,8,128]{2,1,0:T(8,128)}), f32[16,8,128]{2,1,0:T(8,128)S(1)}, u32[]{:S(2)}, u32[]{:S(2)}) async-start(f32[16,8,128]{2,1,0:T(8,128)} %get-tuple-element.10), calls=%async_computation | async-start | bytes 131072 | tf_op jit(solution)/shard_map/all_to_all | solution.py:273
  11.6 0.0 copy-start
  11.6 0.9 %copy-done = f32[8,6144]{1,0:T(8,128)S(1)} copy-done((f32[8,6144]{1,0:T(8,128)S(1)}, f32[8,6144]{1,0:T(8,128)}, u32[]{:S(2)}) %copy-start) | copy-done | bytes 196632
  12.5 2.3 %prepare.1 = (bf16[6144,128]{1,0:T(8,128)(2,1)S(1)}, bf16[32,6144]{1,0:T(8,128)(2,1)S(1)}) custom-call(f32[8,6144]{1,0:T(8,128)S(1)} %copy-done), custom_call_target="tpu_custom_call" | custom-call | flops 4194304 | bytes 4194304 | tf_op jit(solution)/shard_map/prepare/pallas_call | solution.py:274
  14.8 3.9 %all-to-all-done.recv_ref = f32[16,8,128]{2,1,0:T(8,128)S(1)} async-done(((f32[16,8,128]{2,1,0:T(8,128)}), f32[16,8,128]{2,1,0:T(8,128)S(1)}, u32[]{:S(2)}, u32[]{:S(2)}) %all-to-all-start) | async-done | bytes 65568 | tf_op jit(solution)/shard_map/all_to_all | solution.py:273
  18.7 0.0 copy-start.1
  18.7 12.4 %sweep.1 = f32[16,8,128]{2,1,0:T(8,128)S(1)} custom-call(f32[16,8,128]{2,1,0:T(8,128)S(1)} %all-to-all-done.recv_ref, bf16[6144,128]{1,0:T(8,128)(2,1)S(1)} %get-tuple-element.12.ys_ref, bf16[32,6144]{1,0:T(8,128)(2,1)S(1)} %get-tuple-element.13.mt_ref), custom_call_target="tpu_custom_call" | custom-call | flops 10737418240 | bytes 4194304 | tf_op jit(solution)/shard_map/sweep/pallas_call | solution.py:284
  31.1 10.0 %all_to_all.10.recv_ref = f32[16,8,128]{2,1,0:T(8,128)S(1)} all-to-all(f32[16,8,128]{2,1,0:T(8,128)S(1)} %sweep.1), channel_id=1, replica_groups={{0,8,20,28,32,40,52,60,64,72,84,92,96,104,116,124},{4,12,16,24,36,44,48..., dimensions={0} | all-to-all | bytes 131072 | tf_op jit(solution)/shard_map/all_to_all | solution.py:295
  41.0 0.0 copy-done.1
  41.0 0.6 %finish.1 = f32[12,1,1,64]{3,2,1,0:T(1,128)} custom-call(f32[16,8,128]{2,1,0:T(8,128)S(1)} %all_to_all.10.recv_ref, f32[16,128]{1,0:T(8,128)S(1)} %copy-done.1), custom_call_target="tpu_custom_call" | custom-call | tf_op jit(solution)/shard_map/finish/pallas_call | solution.py:296
Async XLA Ops:
  3.1 15.6 %all-to-all-start = ((f32[16,8,128]{2,1,0:T(8,128)}), f32[16,8,128]{2,1,0:T(8,128)S(1)}, u32[]{:S(2)}, u32[]{:S(2)}) async-start(f32[16,8,128]{2,1,0:T(8,128)} %get-tuple-element.10), calls=%async_computation | async-start | bytes 131072 | tf_op jit(solution)/shard_map/all_to_all | solution.py:273
  11.6 0.9 %copy-start = (f32[8,6144]{1,0:T(8,128)S(1)}, f32[8,6144]{1,0:T(8,128)}, u32[]{:S(2)}) copy-start(f32[8,6144]{1,0:T(8,128)} %get-tuple-element.11.pv_ref) | copy-start | bytes 589828
  18.7 22.3 %copy-start.1 = (f32[16,128]{1,0:T(8,128)S(1)}, f32[16,128]{1,0:T(8,128)}, u32[]{:S(2)}) copy-start(f32[16,128]{1,0:T(8,128)} %get-tuple-element.14.own_ref) | copy-start | bytes 24580

commit v2 on v1

--- a/solution.py
+++ b/solution.py
@@ -15,7 +15,6 @@
 GRID = 16.0
 LANES = 128
 CAP = 64
-STEP = 2048
 VMEM = 44 << 20
 
 
@@ -146,7 +145,7 @@
     wr_ref[26:32, :] = jnp.ones((6, n), F32)
 
 
-def sweep_kernel(recv_ref, ys_ref, mt_ref, out_ref, act_ref, res_ref, wq_ref, wr_ref, wqb_ref, wrb_ref):
+def sweep_kernel(recv_ref, ys_ref, mt_ref, out_ref, act_ref, res_ref, wq_ref, wr_ref, wa_ref, wb_ref):
     lists = recv_ref.shape[0]
     stars = ys_ref.shape[0]
     lane = lax.broadcasted_iota(jnp.int32, (8, LANES), 1)
@@ -164,49 +163,38 @@
         total = total + jnp.max(recv_ref[k, 6:7, :].astype(jnp.int32))
     size = wq_ref.shape[1]
     fill_weights(act_ref[0:3, 0:size], act_ref[3:6, 0:size], wq_ref, wr_ref)
-    wqb_ref[...] = wq_ref[...].astype(BF16)
-    wrb_ref[...] = wr_ref[...].astype(BF16)
-
-    def tile(a, width):
-        cols = pl.ds(a, width)
-        w = jnp.concatenate([wqb_ref[:, cols], wrb_ref[:, cols]], axis=1)
-
-        def body(i, carry):
-            high, low = carry
-            o = pl.multiple_of(i * STEP, STEP)
-            qr = jnp.dot(ys_ref[pl.ds(o, STEP), :], w, preferred_element_type=F32)
-            q, rw = qr[:, :width], qr[:, width:]
+    for w in (wa_ref, wb_ref):
+        w[0] = wq_ref[...].astype(BF16)
+        w[1] = wr_ref[...].astype(BF16)
+
+    def dot(a, b):
+        return jnp.dot(a, b, preferred_element_type=F32)
+
+    def tile(t, _):
+        cols = pl.ds(pl.multiple_of(t * LANES, LANES), LANES)
+        half = stars // 2
+        parts = []
+        for h, w in enumerate((wa_ref, wb_ref)):
+            rows = slice(h * half, (h + 1) * half)
+            qr = dot(ys_ref[rows, :], jnp.concatenate([w[0, :, cols], w[1, :, cols]], axis=1))
+            q, rw = qr[:, :LANES], qr[:, LANES:]
             inv = lax.rsqrt(q)
             inv2 = inv * inv
             s = inv * inv2
             st = jnp.concatenate([s, s * inv2 * rw], axis=1)
             hi = st.astype(BF16)
             lo = (st - hi.astype(F32)).astype(BF16)
-            high = high + jnp.dot(mt_ref[:, pl.ds(o, STEP)], hi, preferred_element_type=F32)
-            low = low + jnp.dot(mt_ref[0:16, pl.ds(o, STEP)], lo, preferred_element_type=F32)
-            return high, low
-
-        zero = jnp.zeros((32, 2 * width), F32), jnp.zeros((16, 2 * width), F32)
-        high, low = lax.fori_loop(0, stars // STEP, body, zero)
+            parts.append((dot(mt_ref[:, rows], hi), dot(mt_ref[0:16, rows], lo)))
+        high = parts[0][0] + parts[1][0]
+        low = parts[0][1] + parts[1][1]
         x = (high[16:24] + low[8:16]) + (high[8:16] + low[0:8]) + high[0:8]
-        s, t = x[:, :width], x[:, width:]
+        s, t = x[:, :LANES], x[:, LANES:]
         p, v = act_ref[0:3, cols], act_ref[3:6, cols]
         res_ref[0:3, cols] = s[0:3] - p * s[6:7]
         res_ref[3:6, cols] = s[3:6] - v * s[6:7] - 3.0 * (t[0:3] - p * t[6:7])
-
-    tiles = (total + (LANES - 1)) >> 7
-    pairs = tiles >> 1
-
-    def two(t, _):
-        tile(pl.multiple_of(t * 2 * LANES, LANES), 2 * LANES)
         return 0
 
-    def one(t, _):
-        tile(pl.multiple_of(t * LANES, LANES), LANES)
-        return 0
-
-    lax.fori_loop(0, pairs, two, 0)
-    lax.fori_loop(2 * pairs, tiles, one, 0)
+    lax.fori_loop(0, (total + (LANES - 1)) >> 7, tile, 0)
     for k in range(lists):
         shift = offsets[k] & (LANES - 1)
         o = pl.multiple_of((offsets[k] >> 7) * LANES, LANES)
@@ -287,7 +275,7 @@
         in_specs=[vmem] * 3,
         scratch_shapes=[pltpu.VMEM((8, size + LANES), F32)] * 2
         + [pltpu.VMEM((LANES, size), F32)] * 2
-        + [pltpu.VMEM((LANES, size), BF16)] * 2,
+        + [pltpu.VMEM((2, LANES, size), BF16)] * 2,
         compiler_params=params(),
         cost_estimate=pl.CostEstimate(flops=10 << 30, bytes_accessed=4 << 20, transcendentals=0),
         name="sweep",

time: 41.9 us -> 40.4 us (0.964)
  the two profiles are of different devices: /device:TPU:17 before, /device:TPU:1 now
where the time goes in v2:
time: 40.4 us; the launch traced here: 40.2 us
  Pallas kernels  15.4 us (38%)
  blocking collectives  9.97 us (25%)
  starting transfers between devices  9.3 us (23%)
  waiting for transfers between devices  3.86 us (10%)
  local copies, waits for them, and re-layouts  0.93 us (2%)
  between operations  0.68 us (2%)
    pallas_call x1, Pallas kernels, on_device(): pl.pallas_call(sweep_kernel, out_shape=jax.ShapeDtypeStruct((lists, 8, LA...  10 us
    all_to_all x1, blocking collectives, on_device(): lax.all_to_all(part, axes, 0, 0, axis_index_groups=groups, tiled=True)  9.97 us
    all_to_all x1, starting transfers between devices, on_device(): lax.all_to_all(send, axes, 0, 0, axis_index_groups=groups, tiled=True)  9.3 us
    all_to_all x1, waiting for transfers between devices, on_device(): lax.all_to_all(send, axes, 0, 0, axis_index_groups=groups, tiled=True)  3.86 us
    pallas_call x1, Pallas kernels, on_device(): pl.pallas_call(select_kernel, out_shape=(jax.ShapeDtypeStruct((lists, 8,...  2.48 us
    pallas_call x1, Pallas kernels, on_device(): pl.pallas_call(prepare_kernel, out_shape=(jax.ShapeDtypeStruct((n, LANES)...  2.28 us
    unnamed x4, local copies, waits for them, and re-layouts  0.93 us
  transfers between devices with their start and end apart: 1, of which 1 were waited for; matrix products, arithmetic and copies ran while one was open for 0% of the time, Pallas kernels for 6%

profile of v2, /device:TPU:1, one launch (start us, length us, event | category | flops | bytes accessed | tf_op | source)
XLA Modules:
  0.0 40.2 jit_solution(11939649630017003120)
XLA Ops:
  0.7 2.5 %select.1 = (f32[16,8,128]{2,1,0:T(8,128)}, f32[16,128]{1,0:T(8,128)}, f32[8,6144]{1,0:T(8,128)}) custom-call(s32[1,1,64]{2,1,0:T(1,128)} %idx_hbm.1, s32[1,1]{1,0:T(1,128)S(6)} %copy.9.cnt_hbm, f32[3,6144]{1,0:T(4,128)} %pos_hbm.1, f32[3,6144]{1,0:T(4,128)} %vel_hbm.1, f32[3,6144]{1,0:T(4,128)} %acc_hbm.1, f32[3,6144]{1,0:T(4,128)} %jerk_hbm.1, ...), custom_call_target="tpu_custom_call" | custom-call | flops 1048576 | bytes 1048576 | tf_op jit(solution)/shard_map/select/pallas_call | solution.py:241
  3.1 9.3 %all-to-all-start = ((f32[16,8,128]{2,1,0:T(8,128)}), f32[16,8,128]{2,1,0:T(8,128)S(1)}, u32[]{:S(2)}, u32[]{:S(2)}) async-start(f32[16,8,128]{2,1,0:T(8,128)} %get-tuple-element.10), calls=%async_computation | async-start | bytes 131072 | tf_op jit(solution)/shard_map/all_to_all | solution.py:261
  12.4 0.0 copy-start
  12.4 0.9 %copy-done = f32[8,6144]{1,0:T(8,128)S(1)} copy-done((f32[8,6144]{1,0:T(8,128)S(1)}, f32[8,6144]{1,0:T(8,128)}, u32[]{:S(2)}) %copy-start) | copy-done | bytes 196632
  13.4 2.3 %prepare.1 = (bf16[6144,128]{1,0:T(8,128)(2,1)S(1)}, bf16[32,6144]{1,0:T(8,128)(2,1)S(1)}) custom-call(f32[8,6144]{1,0:T(8,128)S(1)} %copy-done), custom_call_target="tpu_custom_call" | custom-call | flops 4194304 | bytes 4194304 | tf_op jit(solution)/shard_map/prepare/pallas_call | solution.py:262
  15.7 3.9 %all-to-all-done.recv_ref = f32[16,8,128]{2,1,0:T(8,128)S(1)} async-done(((f32[16,8,128]{2,1,0:T(8,128)}), f32[16,8,128]{2,1,0:T(8,128)S(1)}, u32[]{:S(2)}, u32[]{:S(2)}) %all-to-all-start) | async-done | bytes 65568 | tf_op jit(solution)/shard_map/all_to_all | solution.py:261
  19.5 0.0 copy-start.1
  19.5 10.0 %sweep.1 = f32[16,8,128]{2,1,0:T(8,128)S(1)} custom-call(f32[16,8,128]{2,1,0:T(8,128)S(1)} %all-to-all-done.recv_ref, bf16[6144,128]{1,0:T(8,128)(2,1)S(1)} %get-tuple-element.12.ys_ref, bf16[32,6144]{1,0:T(8,128)(2,1)S(1)} %get-tuple-element.13.mt_ref), custom_call_target="tpu_custom_call" | custom-call | flops 10737418240 | bytes 4194304 | tf_op jit(solution)/shard_map/sweep/pallas_call | solution.py:272
  29.6 10.0 %all_to_all.10.recv_ref = f32[16,8,128]{2,1,0:T(8,128)S(1)} all-to-all(f32[16,8,128]{2,1,0:T(8,128)S(1)} %sweep.1), channel_id=1, replica_groups={{0,8,20,28,32,40,52,60,64,72,84,92,96,104,116,124},{4,12,16,24,36,44,48..., dimensions={0} | all-to-all | bytes 131072 | tf_op jit(solution)/shard_map/all_to_all | solution.py:283
  39.5 0.0 copy-done.1
  39.5 0.6 %finish.1 = f32[12,1,1,64]{3,2,1,0:T(1,128)} custom-call(f32[16,8,128]{2,1,0:T(8,128)S(1)} %all_to_all.10.recv_ref, f32[16,128]{1,0:T(8,128)S(1)} %copy-done.1), custom_call_target="tpu_custom_call" | custom-call | tf_op jit(solution)/shard_map/finish/pallas_call | solution.py:284
Async XLA Ops:
  3.1 16.4 %all-to-all-start = ((f32[16,8,128]{2,1,0:T(8,128)}), f32[16,8,128]{2,1,0:T(8,128)S(1)}, u32[]{:S(2)}, u32[]{:S(2)}) async-start(f32[16,8,128]{2,1,0:T(8,128)} %get-tuple-element.10), calls=%async_computation | async-start | bytes 131072 | tf_op jit(solution)/shard_map/all_to_all | solution.py:261
  12.4 0.9 %copy-start = (f32[8,6144]{1,0:T(8,128)S(1)}, f32[8,6144]{1,0:T(8,128)}, u32[]{:S(2)}) copy-start(f32[8,6144]{1,0:T(8,128)} %get-tuple-element.11.pv_ref) | copy-start | bytes 589828
  19.5 20.0 %copy-start.1 = (f32[16,128]{1,0:T(8,128)S(1)}, f32[16,128]{1,0:T(8,128)}, u32[]{:S(2)}) copy-start(f32[16,128]{1,0:T(8,128)} %get-tuple-element.14.own_ref) | copy-start | bytes 24580

commit v3 on v2

--- a/solution.py
+++ b/solution.py
@@ -56,7 +56,7 @@
 
 
 def select_kernel(
-    idx_hbm, cnt_hbm, pos_hbm, vel_hbm, acc_hbm, jerk_hbm, mass_hbm, lev_hbm,
+    cnt_hbm, idx_hbm, pos_hbm, vel_hbm, acc_hbm, jerk_hbm, mass_hbm, lev_hbm,
     send_ref, own_ref, pv_ref, idx, cnt, pos, vel, acc, jerk, mass, lev, table, sem,
 ):
     pairs = (
@@ -170,31 +170,60 @@
     def dot(a, b):
         return jnp.dot(a, b, preferred_element_type=F32)
 
+    def strengths(qr):
+        q, rw = qr[:, :LANES], qr[:, LANES:]
+        inv = lax.rsqrt(q)
+        inv2 = inv * inv
+        s = inv * inv2
+        st = jnp.concatenate([s, s * inv2 * rw], axis=1)
+        hi = st.astype(BF16)
+        return hi, (st - hi.astype(F32)).astype(BF16)
+
+    def store(cols, s, t):
+        p, v = act_ref[0:3, cols], act_ref[3:6, cols]
+        res_ref[0:3, cols] = s[0:3] - p * s[6:7]
+        res_ref[3:6, cols] = s[3:6] - v * s[6:7] - 3.0 * (t[0:3] - p * t[6:7])
+
     def tile(t, _):
         cols = pl.ds(pl.multiple_of(t * LANES, LANES), LANES)
         half = stars // 2
-        parts = []
+        high, low = jnp.zeros((32, 2 * LANES), F32), jnp.zeros((16, 2 * LANES), F32)
         for h, w in enumerate((wa_ref, wb_ref)):
             rows = slice(h * half, (h + 1) * half)
-            qr = dot(ys_ref[rows, :], jnp.concatenate([w[0, :, cols], w[1, :, cols]], axis=1))
-            q, rw = qr[:, :LANES], qr[:, LANES:]
-            inv = lax.rsqrt(q)
-            inv2 = inv * inv
-            s = inv * inv2
-            st = jnp.concatenate([s, s * inv2 * rw], axis=1)
-            hi = st.astype(BF16)
-            lo = (st - hi.astype(F32)).astype(BF16)
-            parts.append((dot(mt_ref[:, rows], hi), dot(mt_ref[0:16, rows], lo)))
-        high = parts[0][0] + parts[1][0]
-        low = parts[0][1] + parts[1][1]
+            hi, lo = strengths(dot(ys_ref[rows, :], jnp.concatenate([w[0, :, cols], w[1, :, cols]], axis=1)))
+            high = high + dot(mt_ref[:, rows], hi)
+            low = low + dot(mt_ref[0:16, rows], lo)
         x = (high[16:24] + low[8:16]) + (high[8:16] + low[0:8]) + high[0:8]
-        s, t = x[:, :LANES], x[:, LANES:]
-        p, v = act_ref[0:3, cols], act_ref[3:6, cols]
-        res_ref[0:3, cols] = s[0:3] - p * s[6:7]
-        res_ref[3:6, cols] = s[3:6] - v * s[6:7] - 3.0 * (t[0:3] - p * t[6:7])
+        store(cols, x[:, :LANES], x[:, LANES:])
         return 0
 
-    lax.fori_loop(0, (total + (LANES - 1)) >> 7, tile, 0)
+    def narrow_tile(t, _):
+        cols = pl.ds(pl.multiple_of(t * LANES, LANES), LANES)
+        half = stars // 2
+        first = lax.broadcasted_iota(jnp.int32, (LANES, LANES), 1) < LANES // 2
+        weights = []
+        for ref in (wq_ref, wr_ref):
+            w = jnp.where(first, ref[:, cols], 0.0)
+            weights.append(jnp.concatenate([w, pltpu.roll(w, LANES // 2, 1)], axis=0))
+        w = jnp.concatenate(weights, axis=1).astype(BF16)
+        high, low = jnp.zeros((64, 2 * LANES), F32), jnp.zeros((32, 2 * LANES), F32)
+        for h in range(2):
+            a = slice(h * half // 2, (h + 1) * half // 2)
+            b = slice(half + h * half // 2, half + (h + 1) * half // 2)
+            hi, lo = strengths(dot(jnp.concatenate([ys_ref[a, :], ys_ref[b, :]], axis=1), w))
+            high = high + dot(jnp.concatenate([mt_ref[:, a], mt_ref[:, b]], axis=0), hi)
+            low = low + dot(jnp.concatenate([mt_ref[0:16, a], mt_ref[0:16, b]], axis=0), lo)
+        x = (high[16:24] + low[8:16]) + (high[8:16] + low[0:8]) + high[0:8]
+        y = (high[48:56] + low[24:32]) + (high[40:48] + low[16:24]) + high[32:40]
+        s = x[:, :LANES] + pltpu.roll(y[:, :LANES], LANES // 2, 1)
+        t = x[:, LANES:] + pltpu.roll(y[:, LANES:], LANES // 2, 1)
+        store(cols, s, t)
+        return 0
+
+    rest = total & (LANES - 1)
+    whole = (total >> 7) + jnp.where(rest > LANES // 2, 1, 0)
+    lax.fori_loop(0, whole, tile, 0)
+    lax.fori_loop(whole, (total + (LANES - 1)) >> 7, narrow_tile, 0)
     for k in range(lists):
         shift = offsets[k] & (LANES - 1)
         o = pl.multiple_of((offsets[k] >> 7) * LANES, LANES)
@@ -250,13 +279,16 @@
         + [pltpu.VMEM((3, n), F32)] * 4
         + [pltpu.VMEM((1, n), F32), pltpu.VMEM((1, n), jnp.int32), pltpu.VMEM((16, n), F32)]
         + [pltpu.SemaphoreType.DMA((8,))],
-        compiler_params=params(60 << 20),
+        compiler_params=params(),
         cost_estimate=pl.CostEstimate(flops=1 << 20, bytes_accessed=1 << 20, transcendentals=0),
         name="select",
-    )(
-        active_index, active_count, field_pos, field_vel, field_acc, field_jerk,
-        field_mass.reshape(1, n), levels.reshape(1, n),
-    )
+    )(active_count, *[
+        pltpu.with_memory_space_constraint(x, pltpu.HBM)
+        for x in (
+            active_index, field_pos, field_vel, field_acc, field_jerk,
+            field_mass.reshape(1, n), levels.reshape(1, n),
+        )
+    ])
     axes = ("blk", "act")
     recv = lax.all_to_all(send, axes, 0, 0, axis_index_groups=groups, tiled=True)
     ys, mt = pl.pallas_call(

time: 40.4 us -> 40.1 us (level)
  waiting for transfers between devices: 3.86 us -> 4.79 us
  local copies, waits for them, and re-layouts: 0.93 us -> 0 us
    all_to_all x1, waiting for transfers between devices: 3.86 us -> 4.79 us  [on_device(): lax.all_to_all(send, axes, 0, 0, axis_index_groups=groups, tiled=True)]
    unnamed x4 -> x0, local copies, waits for them, and re-layouts: 0.93 us -> none
where the time goes in v3:
time: 40.1 us
  Pallas kernels  15.4 us (38%)
  blocking collectives  9.93 us (25%)
  starting transfers between devices  9.3 us (23%)
  waiting for transfers between devices  4.79 us (12%)
  between operations  0.68 us (2%)
    pallas_call x1, Pallas kernels, on_device(): pl.pallas_call(sweep_kernel, out_shape=jax.ShapeDtypeStruct((lists, 8, LA...  10.1 us
    all_to_all x1, blocking collectives, on_device(): lax.all_to_all(part, axes, 0, 0, axis_index_groups=groups, tiled=True)  9.93 us
    all_to_all x1, starting transfers between devices, on_device(): lax.all_to_all(send, axes, 0, 0, axis_index_groups=groups, tiled=True)  9.3 us
    all_to_all x1, waiting for transfers between devices, on_device(): lax.all_to_all(send, axes, 0, 0, axis_index_groups=groups, tiled=True)  4.79 us
    pallas_call x1, Pallas kernels, on_device(): pl.pallas_call(select_kernel, out_shape=(jax.ShapeDtypeStruct((lists, 8,...  2.39 us
    pallas_call x1, Pallas kernels, on_device(): pl.pallas_call(prepare_kernel, out_shape=(jax.ShapeDtypeStruct((n, LANES)...  2.28 us
  transfers between devices with their start and end apart: 1, of which 1 were waited for; matrix products, arithmetic and copies ran while one was open for 0% of the time, Pallas kernels for 6%

profile of v3, /device:TPU:1, one launch (start us, length us, event | category | flops | bytes accessed | tf_op | source)
XLA Modules:
  0.0 40.1 jit_solution(11279409794438314076)
XLA Ops:
  0.7 2.4 %select.1 = (f32[16,8,128]{2,1,0:T(8,128)}, f32[16,128]{1,0:T(8,128)S(1)}, f32[8,6144]{1,0:T(8,128)S(1)}) custom-call(s32[1,1]{1,0:T(1,128)S(6)} %copy.9.cnt_hbm, s32[1,1,64]{2,1,0:T(1,128)} %idx_hbm.1, f32[3,6144]{1,0:T(4,128)} %pos_hbm.1, f32[3,6144]{1,0:T(4,128)} %vel_hbm.1, f32[3,6144]{1,0:T(4,128)} %acc_hbm.1, f32[3,6144]{1,0:T(4,128)} %jerk_hbm.1, ...), custom_call_target="tpu_custom_call" | custom-call | flops 1048576 | bytes 1048576 | tf_op jit(solution)/shard_map/select/pallas_call | solution.py:270
  3.1 9.3 %all-to-all-start = ((f32[16,8,128]{2,1,0:T(8,128)}), f32[16,8,128]{2,1,0:T(8,128)S(1)}, u32[]{:S(2)}, u32[]{:S(2)}) async-start(f32[16,8,128]{2,1,0:T(8,128)} %get-tuple-element.10), calls=%async_computation | async-start | bytes 131072 | tf_op jit(solution)/shard_map/all_to_all | solution.py:293
  12.4 2.3 %prepare.1 = (bf16[6144,128]{1,0:T(8,128)(2,1)S(1)}, bf16[32,6144]{1,0:T(8,128)(2,1)S(1)}) custom-call(f32[8,6144]{1,0:T(8,128)S(1)} %get-tuple-element.11.pv_ref), custom_call_target="tpu_custom_call" | custom-call | flops 4194304 | bytes 4194304 | tf_op jit(solution)/shard_map/prepare/pallas_call | solution.py:294
  14.6 4.8 %all-to-all-done.recv_ref = f32[16,8,128]{2,1,0:T(8,128)S(1)} async-done(((f32[16,8,128]{2,1,0:T(8,128)}), f32[16,8,128]{2,1,0:T(8,128)S(1)}, u32[]{:S(2)}, u32[]{:S(2)}) %all-to-all-start) | async-done | bytes 65568 | tf_op jit(solution)/shard_map/all_to_all | solution.py:293
  19.4 10.1 %sweep.1 = f32[16,8,128]{2,1,0:T(8,128)S(1)} custom-call(f32[16,8,128]{2,1,0:T(8,128)S(1)} %all-to-all-done.recv_ref, bf16[6144,128]{1,0:T(8,128)(2,1)S(1)} %get-tuple-element.12.ys_ref, bf16[32,6144]{1,0:T(8,128)(2,1)S(1)} %get-tuple-element.13.mt_ref), custom_call_target="tpu_custom_call" | custom-call | flops 10737418240 | bytes 4194304 | tf_op jit(solution)/shard_map/sweep/pallas_call | solution.py:304
  29.6 9.9 %all_to_all.10.recv_ref = f32[16,8,128]{2,1,0:T(8,128)S(1)} all-to-all(f32[16,8,128]{2,1,0:T(8,128)S(1)} %sweep.1), channel_id=1, replica_groups={{0,8,20,28,32,40,52,60,64,72,84,92,96,104,116,124},{4,12,16,24,36,44,48..., dimensions={0} | all-to-all | bytes 131072 | tf_op jit(solution)/shard_map/all_to_all | solution.py:315
  39.5 0.6 %finish.1 = f32[12,1,1,64]{3,2,1,0:T(1,128)} custom-call(f32[16,8,128]{2,1,0:T(8,128)S(1)} %all_to_all.10.recv_ref, f32[16,128]{1,0:T(8,128)S(1)} %get-tuple-element.14.own_ref), custom_call_target="tpu_custom_call" | custom-call | tf_op jit(solution)/shard_map/finish/pallas_call | solution.py:316
Async XLA Ops:
  3.1 16.4 %all-to-all-start = ((f32[16,8,128]{2,1,0:T(8,128)}), f32[16,8,128]{2,1,0:T(8,128)S(1)}, u32[]{:S(2)}, u32[]{:S(2)}) async-start(f32[16,8,128]{2,1,0:T(8,128)} %get-tuple-element.10), calls=%async_computation | async-start | bytes 131072 | tf_op jit(solution)/shard_map/all_to_all | solution.py:293

commit v4 on v3

--- a/solution.py
+++ b/solution.py
@@ -69,8 +69,7 @@
     for copy in copies:
         copy.wait()
     level = lev[...]
-    period = jnp.left_shift(jnp.ones_like(level), 4 - level)
-    e = lax.rem(jnp.full_like(level, NOW), period).astype(F32) * TICK
+    e = (NOW & (jnp.left_shift(jnp.ones_like(level), 4 - level) - 1)).astype(F32) * TICK
     x, u, a, j = pos[...], vel[...], acc[...], jerk[...]
     p = x + e * (u + e * (a * 0.5 + e * j / 6.0))
     v = u + e * (a + e * j * 0.5)
@@ -145,27 +144,36 @@
     wr_ref[26:32, :] = jnp.ones((6, n), F32)
 
 
-def sweep_kernel(recv_ref, ys_ref, mt_ref, out_ref, act_ref, res_ref, wq_ref, wr_ref, wa_ref, wb_ref):
+def sweep_kernel(recv_ref, ys_ref, mt_ref, out_ref, act_ref, res_ref, wq_ref, wr_ref, w_ref):
     lists = recv_ref.shape[0]
     stars = ys_ref.shape[0]
     lane = lax.broadcasted_iota(jnp.int32, (8, LANES), 1)
     act_ref[...] = jnp.zeros(act_ref.shape, F32)
     offsets = []
     total = jnp.int32(0)
+    chunk = jnp.zeros((8, LANES), F32)
     for k in range(lists):
-        x = recv_ref[k]
         offsets.append(total)
         shift = total & (LANES - 1)
         o = pl.multiple_of((total >> 7) * LANES, LANES)
-        x = pltpu.roll(x, shift, 1)
-        act_ref[:, pl.ds(o, LANES)] += jnp.where(lane >= shift, x, 0.0)
-        act_ref[:, pl.ds(o + LANES, LANES)] += jnp.where(lane < shift, x, 0.0)
+        x = pltpu.roll(recv_ref[k], shift, 1)
+        chunk = chunk + jnp.where(lane >= shift, x, 0.0)
+        act_ref[:, pl.ds(o, LANES)] = chunk
         total = total + jnp.max(recv_ref[k, 6:7, :].astype(jnp.int32))
+        full = (total >> 7) * LANES > o
+        chunk = jnp.where(full, jnp.where(lane < shift, x, 0.0), chunk)
+    act_ref[:, pl.ds(pl.multiple_of((total >> 7) * LANES, LANES), LANES)] = chunk
     size = wq_ref.shape[1]
-    fill_weights(act_ref[0:3, 0:size], act_ref[3:6, 0:size], wq_ref, wr_ref)
-    for w in (wa_ref, wb_ref):
-        w[0] = wq_ref[...].astype(BF16)
-        w[1] = wr_ref[...].astype(BF16)
+    common = size * 5 // 8
+
+    def ready(lo, hi):
+        cols = slice(lo, hi)
+        fill_weights(act_ref[0:3, cols], act_ref[3:6, cols], wq_ref.at[:, cols], wr_ref.at[:, cols])
+        w_ref[0, :, cols] = wq_ref[:, cols].astype(BF16)
+        w_ref[1, :, cols] = wr_ref[:, cols].astype(BF16)
+
+    ready(0, common)
+    pl.when(total > common)(lambda: ready(common, size))
 
     def dot(a, b):
         return jnp.dot(a, b, preferred_element_type=F32)
@@ -188,9 +196,10 @@
         cols = pl.ds(pl.multiple_of(t * LANES, LANES), LANES)
         half = stars // 2
         high, low = jnp.zeros((32, 2 * LANES), F32), jnp.zeros((16, 2 * LANES), F32)
-        for h, w in enumerate((wa_ref, wb_ref)):
+        w = jnp.concatenate([w_ref[0, :, cols], w_ref[1, :, cols]], axis=1)
+        for h in range(2):
             rows = slice(h * half, (h + 1) * half)
-            hi, lo = strengths(dot(ys_ref[rows, :], jnp.concatenate([w[0, :, cols], w[1, :, cols]], axis=1)))
+            hi, lo = strengths(dot(ys_ref[rows, :], w))
             high = high + dot(mt_ref[:, rows], hi)
             low = low + dot(mt_ref[0:16, rows], lo)
         x = (high[16:24] + low[8:16]) + (high[8:16] + low[0:8]) + high[0:8]
@@ -307,7 +316,7 @@
         in_specs=[vmem] * 3,
         scratch_shapes=[pltpu.VMEM((8, size + LANES), F32)] * 2
         + [pltpu.VMEM((LANES, size), F32)] * 2
-        + [pltpu.VMEM((2, LANES, size), BF16)] * 2,
+        + [pltpu.VMEM((2, LANES, size), BF16)],
         compiler_params=params(),
         cost_estimate=pl.CostEstimate(flops=10 << 30, bytes_accessed=4 << 20, transcendentals=0),
         name="sweep",

time: 40.1 us -> 40.4 us (level)
  the two profiles are of different devices: /device:TPU:1 before, /device:TPU:25 now
where the time goes in v4:
time: 40.4 us; the launch traced here: 40.1 us
  Pallas kernels  16.2 us (40%)
  blocking collectives  9.94 us (25%)
  starting transfers between devices  8.47 us (21%)
  waiting for transfers between devices  4.79 us (12%)
  between operations  0.68 us (2%)
    pallas_call x1, Pallas kernels, on_device(): pl.pallas_call(sweep_kernel, out_shape=jax.ShapeDtypeStruct((lists, 8, LA...  11.2 us
    all_to_all x1, blocking collectives, on_device(): lax.all_to_all(part, axes, 0, 0, axis_index_groups=groups, tiled=True)  9.94 us
    all_to_all x1, starting transfers between devices, on_device(): lax.all_to_all(send, axes, 0, 0, axis_index_groups=groups, tiled=True)  8.47 us
    all_to_all x1, waiting for transfers between devices, on_device(): lax.all_to_all(send, axes, 0, 0, axis_index_groups=groups, tiled=True)  4.79 us
    pallas_call x1, Pallas kernels, on_device(): pl.pallas_call(prepare_kernel, out_shape=(jax.ShapeDtypeStruct((n, LANES)...  2.28 us
    pallas_call x1, Pallas kernels, on_device(): pl.pallas_call(select_kernel, out_shape=(jax.ShapeDtypeStruct((lists, 8,...  2.18 us
  transfers between devices with their start and end apart: 1, of which 1 were waited for; matrix products, arithmetic and copies ran while one was open for 0% of the time, Pallas kernels for 6%

profile of v4, /device:TPU:25, one launch (start us, length us, event | category | flops | bytes accessed | tf_op | source)
XLA Modules:
  0.0 40.1 jit_solution(7823600229495935739)
XLA Ops:
  0.7 2.2 %select.1 = (f32[16,8,128]{2,1,0:T(8,128)}, f32[16,128]{1,0:T(8,128)S(1)}, f32[8,6144]{1,0:T(8,128)S(1)}) custom-call(s32[1,1]{1,0:T(1,128)S(6)} %copy.9.cnt_hbm, s32[1,1,64]{2,1,0:T(1,128)} %idx_hbm.1, f32[3,6144]{1,0:T(4,128)} %pos_hbm.1, f32[3,6144]{1,0:T(4,128)} %vel_hbm.1, f32[3,6144]{1,0:T(4,128)} %acc_hbm.1, f32[3,6144]{1,0:T(4,128)} %jerk_hbm.1, ...), custom_call_target="tpu_custom_call" | custom-call | flops 1048576 | bytes 1048576 | tf_op jit(solution)/shard_map/select/pallas_call | solution.py:279
  2.8 8.5 %all-to-all-start = ((f32[16,8,128]{2,1,0:T(8,128)}), f32[16,8,128]{2,1,0:T(8,128)S(1)}, u32[]{:S(2)}, u32[]{:S(2)}) async-start(f32[16,8,128]{2,1,0:T(8,128)} %get-tuple-element.10), calls=%async_computation | async-start | bytes 131072 | tf_op jit(solution)/shard_map/all_to_all | solution.py:302
  11.3 2.3 %prepare.1 = (bf16[6144,128]{1,0:T(8,128)(2,1)S(1)}, bf16[32,6144]{1,0:T(8,128)(2,1)S(1)}) custom-call(f32[8,6144]{1,0:T(8,128)S(1)} %get-tuple-element.11.pv_ref), custom_call_target="tpu_custom_call" | custom-call | flops 4194304 | bytes 4194304 | tf_op jit(solution)/shard_map/prepare/pallas_call | solution.py:303
  13.6 4.8 %all-to-all-done.recv_ref = f32[16,8,128]{2,1,0:T(8,128)S(1)} async-done(((f32[16,8,128]{2,1,0:T(8,128)}), f32[16,8,128]{2,1,0:T(8,128)S(1)}, u32[]{:S(2)}, u32[]{:S(2)}) %all-to-all-start) | async-done | bytes 65568 | tf_op jit(solution)/shard_map/all_to_all | solution.py:302
  18.4 11.2 %sweep.1 = f32[16,8,128]{2,1,0:T(8,128)S(1)} custom-call(f32[16,8,128]{2,1,0:T(8,128)S(1)} %all-to-all-done.recv_ref, bf16[6144,128]{1,0:T(8,128)(2,1)S(1)} %get-tuple-element.12.ys_ref, bf16[32,6144]{1,0:T(8,128)(2,1)S(1)} %get-tuple-element.13.mt_ref), custom_call_target="tpu_custom_call" | custom-call | flops 10737418240 | bytes 4194304 | tf_op jit(solution)/shard_map/sweep/pallas_call | solution.py:313
  29.6 9.9 %all_to_all.10.recv_ref = f32[16,8,128]{2,1,0:T(8,128)S(1)} all-to-all(f32[16,8,128]{2,1,0:T(8,128)S(1)} %sweep.1), channel_id=1, replica_groups={{0,8,20,28,32,40,52,60,64,72,84,92,96,104,116,124},{4,12,16,24,36,44,48..., dimensions={0} | all-to-all | bytes 131072 | tf_op jit(solution)/shard_map/all_to_all | solution.py:324
  39.5 0.6 %finish.1 = f32[12,1,1,64]{3,2,1,0:T(1,128)} custom-call(f32[16,8,128]{2,1,0:T(8,128)S(1)} %all_to_all.10.recv_ref, f32[16,128]{1,0:T(8,128)S(1)} %get-tuple-element.14.own_ref), custom_call_target="tpu_custom_call" | custom-call | tf_op jit(solution)/shard_map/finish/pallas_call | solution.py:325
Async XLA Ops:
  2.8 15.6 %all-to-all-start = ((f32[16,8,128]{2,1,0:T(8,128)}), f32[16,8,128]{2,1,0:T(8,128)S(1)}, u32[]{:S(2)}, u32[]{:S(2)}) async-start(f32[16,8,128]{2,1,0:T(8,128)} %get-tuple-element.10), calls=%async_computation | async-start | bytes 131072 | tf_op jit(solution)/shard_map/all_to_all | solution.py:302

commit v5 on v4

--- a/solution.py
+++ b/solution.py
@@ -15,6 +15,7 @@
 GRID = 16.0
 LANES = 128
 CAP = 64
+FINE = 16
 VMEM = 44 << 20
 
 
@@ -101,12 +102,21 @@
     n = pv_ref.shape[1]
     p, v, m = pv_ref[0:3, :], pv_ref[3:6, :], pv_ref[6:7, :]
     (pp, vv), norms = basis(p, v)
+    cc, dn, ce, gn = (split3(x) for x in norms)
+    ones = jnp.ones((4, n), F32)
+    b_ref[0:3, :] = pp[0]
+    b_ref[3:6, :] = vv[0]
+    for t in range(3):
+        b_ref[6 + t : 7 + t, :] = cc[t]
+        b_ref[9 + t : 10 + t, :] = ce[t]
+    b_ref[12:16, :] = ones
     for k, x in enumerate((*pp, *vv)):
-        b_ref[3 * k : 3 * k + 3, :] = x
-    b_ref[18:20, :] = jnp.ones((2, n), F32)
-    for k, x in enumerate(norms):
-        for t, y in enumerate(split3(x)):
-            b_ref[20 + 3 * k + t : 21 + 3 * k + t, :] = y
+        b_ref[FINE + 3 * k : FINE + 3 * k + 3, :] = x
+    b_ref[FINE + 18 : FINE + 20, :] = ones[0:2]
+    for t in range(3):
+        b_ref[FINE + 20 + t : FINE + 21 + t, :] = dn[t]
+        b_ref[FINE + 23 + t : FINE + 24 + t, :] = gn[t]
+    b_ref[FINE + 26 : FINE + 32, :] = jnp.zeros((6, n), F32)
     m_ref[...] = jnp.zeros(m_ref.shape, F32)
     for k, x in enumerate((m * p, m * v)):
         for t, y in enumerate(split3(x)):
@@ -117,8 +127,9 @@
 
     def body(i, _):
         o = pl.multiple_of(i * LANES, LANES)
-        x = b_ref[:, pl.ds(o, LANES)].astype(BF16)
-        ys_ref[pl.ds(o, LANES), :] = jnp.concatenate([x, x, x, x], axis=0).T
+        x = b_ref[0:FINE, pl.ds(o, LANES)].astype(BF16)
+        y = b_ref[FINE : FINE + 32, pl.ds(o, LANES)].astype(BF16)
+        ys_ref[pl.ds(o, LANES), :] = jnp.concatenate([x, y, y, y, x], axis=0).T
         return 0
 
     lax.fori_loop(0, n // LANES, body, 0, unroll=4)
@@ -126,22 +137,30 @@
 
 def fill_weights(p, v, wq_ref, wr_ref):
     n = p.shape[1]
-    (pp, vv), (cc, dn, ce, gn) = basis(p, v)
+    (pp, vv), norms = basis(p, v)
+    cc, dn, ce, gn = norms
+    cc, dn, ce, gn = split3(cc), split3(dn + SOFTEN), split3(ce), split3(gn)
     wq_ref[...] = jnp.zeros(wq_ref.shape, F32)
     wr_ref[...] = jnp.zeros(wr_ref.shape, F32)
-    cc, dn, ce, gn = split3(cc), split3(dn + SOFTEN), split3(ce), split3(gn)
+    ones = jnp.ones((3, n), F32)
+    wq_ref[0:3, :] = -2.0 * pp[0]
+    wr_ref[0:3, :] = -vv[0]
+    wr_ref[3:6, :] = -pp[0]
+    wq_ref[6:9, :] = ones
+    wr_ref[9:12, :] = ones
     for w in range(3):
-        o = 32 * w
+        wq_ref[12 + w : 13 + w, :] = cc[w]
+        wr_ref[12 + w : 13 + w, :] = ce[w]
+        o = FINE + 32 * w
         for k in range(3):
-            wq_ref[o + 3 * k : o + 3 * k + 3, :] = -2.0 * pp[w]
-            wr_ref[o + 3 * k : o + 3 * k + 3, :] = -vv[w]
-            wr_ref[o + 9 + 3 * k : o + 12 + 3 * k, :] = -pp[w]
-        wq_ref[o + 18 : o + 19, :] = cc[w]
-        wq_ref[o + 19 : o + 20, :] = dn[w]
-        wr_ref[o + 18 : o + 19, :] = ce[w]
-        wr_ref[o + 19 : o + 20, :] = gn[w]
-    wq_ref[20:26, :] = jnp.ones((6, n), F32)
-    wr_ref[26:32, :] = jnp.ones((6, n), F32)
+            if w or k:
+                wq_ref[o + 3 * k : o + 3 * k + 3, :] = -2.0 * pp[w]
+                wr_ref[o + 3 * k : o + 3 * k + 3, :] = -vv[w]
+                wr_ref[o + 9 + 3 * k : o + 12 + 3 * k, :] = -pp[w]
+        wq_ref[o + 18 : o + 19, :] = dn[w]
+        wr_ref[o + 18 : o + 19, :] = gn[w]
+    wq_ref[FINE + 20 : FINE + 23, :] = ones
+    wr_ref[FINE + 23 : FINE + 26, :] = ones
 
 
 def sweep_kernel(recv_ref, ys_ref, mt_ref, out_ref, act_ref, res_ref, wq_ref, wr_ref, w_ref):
@@ -304,7 +323,7 @@
         prepare_kernel,
         out_shape=(jax.ShapeDtypeStruct((n, LANES), BF16), jax.ShapeDtypeStruct((32, n), BF16)),
         in_specs=[vmem],
-        scratch_shapes=[pltpu.VMEM((32, n), F32)] * 2,
+        scratch_shapes=[pltpu.VMEM((FINE + 32, n), F32), pltpu.VMEM((32, n), F32)],
         compiler_params=params(),
         cost_estimate=pl.CostEstimate(flops=1 << 22, bytes_accessed=4 << 20, transcendentals=0),
         name="prepare",

time: 40.4 us -> 39.3 us (0.973)
  the two profiles are of different devices: /device:TPU:25 before, /device:TPU:1 now
where the time goes in v5:
time: 39.3 us; the launch traced here: 39 us
  Pallas kernels  14.4 us (37%)
  blocking collectives  9.95 us (25%)
  starting transfers between devices  9.3 us (24%)
  waiting for transfers between devices  4.72 us (12%)
  between operations  0.68 us (2%)
    all_to_all x1, blocking collectives, on_device(): lax.all_to_all(part, axes, 0, 0, axis_index_groups=groups, tiled=True)  9.95 us
    all_to_all x1, starting transfers between devices, on_device(): lax.all_to_all(send, axes, 0, 0, axis_index_groups=groups, tiled=True)  9.3 us
    pallas_call x1, Pallas kernels, on_device(): pl.pallas_call(sweep_kernel, out_shape=jax.ShapeDtypeStruct((lists, 8, LA...  9.22 us
    all_to_all x1, waiting for transfers between devices, on_device(): lax.all_to_all(send, axes, 0, 0, axis_index_groups=groups, tiled=True)  4.72 us
    pallas_call x1, Pallas kernels, on_device(): pl.pallas_call(prepare_kernel, out_shape=(jax.ShapeDtypeStruct((n, LANES)...  2.34 us
    pallas_call x1, Pallas kernels, on_device(): pl.pallas_call(select_kernel, out_shape=(jax.ShapeDtypeStruct((lists, 8,...  2.18 us
  transfers between devices with their start and end apart: 1, of which 1 were waited for; matrix products, arithmetic and copies ran while one was open for 0% of the time, Pallas kernels for 6%

profile of v5, /device:TPU:1, one launch (start us, length us, event | category | flops | bytes accessed | tf_op | source)
XLA Modules:
  0.0 39.0 jit_solution(9322329052051924387)
XLA Ops:
  0.7 2.2 %select.1 = (f32[16,8,128]{2,1,0:T(8,128)}, f32[16,128]{1,0:T(8,128)S(1)}, f32[8,6144]{1,0:T(8,128)S(1)}) custom-call(s32[1,1]{1,0:T(1,128)S(6)} %copy.9.cnt_hbm, s32[1,1,64]{2,1,0:T(1,128)} %idx_hbm.1, f32[3,6144]{1,0:T(4,128)} %pos_hbm.1, f32[3,6144]{1,0:T(4,128)} %vel_hbm.1, f32[3,6144]{1,0:T(4,128)} %acc_hbm.1, f32[3,6144]{1,0:T(4,128)} %jerk_hbm.1, ...), custom_call_target="tpu_custom_call" | custom-call | flops 1048576 | bytes 1048576 | tf_op jit(solution)/shard_map/select/pallas_call | solution.py:298
  2.8 9.3 %all-to-all-start = ((f32[16,8,128]{2,1,0:T(8,128)}), f32[16,8,128]{2,1,0:T(8,128)S(1)}, u32[]{:S(2)}, u32[]{:S(2)}) async-start(f32[16,8,128]{2,1,0:T(8,128)} %get-tuple-element.10), calls=%async_computation | async-start | bytes 131072 | tf_op jit(solution)/shard_map/all_to_all | solution.py:321
  12.1 2.3 %prepare.1 = (bf16[6144,128]{1,0:T(8,128)(2,1)S(1)}, bf16[32,6144]{1,0:T(8,128)(2,1)S(1)}) custom-call(f32[8,6144]{1,0:T(8,128)S(1)} %get-tuple-element.11.pv_ref), custom_call_target="tpu_custom_call" | custom-call | flops 4194304 | bytes 4194304 | tf_op jit(solution)/shard_map/prepare/pallas_call | solution.py:322
  14.5 4.7 %all-to-all-done.recv_ref = f32[16,8,128]{2,1,0:T(8,128)S(1)} async-done(((f32[16,8,128]{2,1,0:T(8,128)}), f32[16,8,128]{2,1,0:T(8,128)S(1)}, u32[]{:S(2)}, u32[]{:S(2)}) %all-to-all-start) | async-done | bytes 65568 | tf_op jit(solution)/shard_map/all_to_all | solution.py:321
  19.2 9.2 %sweep.1 = f32[16,8,128]{2,1,0:T(8,128)S(1)} custom-call(f32[16,8,128]{2,1,0:T(8,128)S(1)} %all-to-all-done.recv_ref, bf16[6144,128]{1,0:T(8,128)(2,1)S(1)} %get-tuple-element.12.ys_ref, bf16[32,6144]{1,0:T(8,128)(2,1)S(1)} %get-tuple-element.13.mt_ref), custom_call_target="tpu_custom_call" | custom-call | flops 10737418240 | bytes 4194304 | tf_op jit(solution)/shard_map/sweep/pallas_call | solution.py:332
  28.5 9.9 %all_to_all.10.recv_ref = f32[16,8,128]{2,1,0:T(8,128)S(1)} all-to-all(f32[16,8,128]{2,1,0:T(8,128)S(1)} %sweep.1), channel_id=1, replica_groups={{0,8,20,28,32,40,52,60,64,72,84,92,96,104,116,124},{4,12,16,24,36,44,48..., dimensions={0} | all-to-all | bytes 131072 | tf_op jit(solution)/shard_map/all_to_all | solution.py:343
  38.4 0.6 %finish.1 = f32[12,1,1,64]{3,2,1,0:T(1,128)} custom-call(f32[16,8,128]{2,1,0:T(8,128)S(1)} %all_to_all.10.recv_ref, f32[16,128]{1,0:T(8,128)S(1)} %get-tuple-element.14.own_ref), custom_call_target="tpu_custom_call" | custom-call | tf_op jit(solution)/shard_map/finish/pallas_call | solution.py:344
Async XLA Ops:
  2.8 16.4 %all-to-all-start = ((f32[16,8,128]{2,1,0:T(8,128)}), f32[16,8,128]{2,1,0:T(8,128)S(1)}, u32[]{:S(2)}, u32[]{:S(2)}) async-start(f32[16,8,128]{2,1,0:T(8,128)} %get-tuple-element.10), calls=%async_computation | async-start | bytes 131072 | tf_op jit(solution)/shard_map/all_to_all | solution.py:321
